TPU v7x, 32 devices: a whole 2x2x4 slice. The times are simulated.
32 devices in a mesh: dp: 8 (over y, x, core), ctx: 4 (over z).
Axes of the slice: x: 2, y: 2, z: 4, core: 2. Of those that a mesh axis runs over, the one named last changes fastest.
Arguments:
- hidden: bfloat16 [8, 1536, 8192], P('dp', 'ctx'), may hold values from -6 to 6
- queries: bfloat16 [8, 1536, 4096], P('dp', 'ctx'), may hold values from -136 to 136
- weights_old: float32 [8192, 1024], P(('dp', 'ctx')), may hold values from -0.0625 to 0.0625
- gradient_old: float32 [8192, 1024], P(('dp', 'ctx')), may hold values from -6 to 6
- first_old: float32 [8192, 1024], P(('dp', 'ctx')), may hold values from -4 to 4
- second_old: float32 [8192, 1024], P(('dp', 'ctx')), may hold values from 0.25 to 4
- old_owner: int32 [32], replicated, may hold values from 0 to 31, each once
- new_owner: int32 [32], replicated, may hold values from 0 to 31, each once
- offsets: int32 [8, 4, 2], P('dp'), may hold values from 0 to 1344, as said below
Outputs:
- weights_new: float32 [1024, 8192], P(('dp', 'ctx'))
- first_new: float32 [1024, 8192], P(('dp', 'ctx'))
- second_new: float32 [1024, 8192], P(('dp', 'ctx'))
- attended: bfloat16 [8, 1536, 4096], P('dp', 'ctx')
Inputs may be any that keep to these rules, and one draw needn't show every extreme that they name: `offsets`: for sequence b and ctx index c the two entries are p * 192 and (7 - p) * 192, where p runs over a permutation of the ctx indices drawn for each sequence. `old_owner`: each block index appears once. `new_owner`: each block index appears once.
All inputs are finite; a program needn't handle non-finite values.
Results may differ from a plain program's by a relative error of at most 0.0055.
The roundings to bfloat16 on the way count: a program that leaves them out, or rounds other values in their place, can miss the bound.
Values may be sent and summed in bfloat16 or wider, within the bound.
A program may use at most 320 MiB of HBM per device.

v0:
```python
import math

import jax
import jax.numpy as jnp
from jax import lax
from jax.sharding import PartitionSpec as P

HEAD = 128
KV_HEADS = 4
Q_HEADS = 32


learn_rate = 0.0003
beta_one = 0.9
beta_two = 0.95
adam_eps = 1e-08
decay_rate = 0.1
step_number = 1000
corr_one = 1.0 - beta_one**step_number
corr_two = 1.0 - beta_two**step_number
rope_base = 500000.0


def adam_step(weights, gradient, first_mom, second_mom):
    first_next = beta_one * first_mom + (1.0 - beta_one) * gradient
    second_next = beta_two * second_mom + (1.0 - beta_two) * gradient * gradient
    direction = first_next / corr_one / (jnp.sqrt(second_next / corr_two) + adam_eps)
    weights_next = weights - learn_rate * (direction + decay_rate * weights)
    return (weights_next, first_next, second_next)


def rotate_keys(key_heads, positions):
    head_dim = key_heads.shape[-1]
    half_dim = head_dim // 2
    exponent = jnp.arange(half_dim, dtype=jnp.float32) * (2.0 / head_dim)
    inv_freq = jnp.power(rope_base, -exponent)
    angles = positions.astype(jnp.float32)[..., None] * inv_freq
    cosine = jnp.cos(angles)[..., None, :]
    sine_part = jnp.sin(angles)[..., None, :]
    first_half = key_heads[..., :half_dim]
    second_half = key_heads[..., half_dim:]
    return jnp.concatenate(
        [
            first_half * cosine - second_half * sine_part,
            second_half * cosine + first_half * sine_part,
        ],
        axis=-1,
    )


def invert(owners):
    devices = owners.shape[0]
    return jnp.zeros((devices,), jnp.int32).at[owners].set(jnp.arange(devices, dtype=jnp.int32))


def relocate(stacked, new_owner, old_owner):
    states_count, row_count, proj_width = stacked.shape
    devices = new_owner.shape[0]
    col_count = proj_width // devices
    outgoing = stacked.reshape(states_count, row_count, devices, col_count).transpose(2, 0, 3, 1)
    outgoing = jnp.take(outgoing, new_owner, axis=0)
    incoming = lax.all_to_all(outgoing, ("dp", "ctx"), split_axis=0, concat_axis=0, tiled=True)
    ordered = jnp.take(incoming, invert(old_owner), axis=0)
    return ordered.transpose(1, 2, 0, 3).reshape(states_count, col_count, devices * row_count)


def shards(
    hidden, queries, weights_old, gradient_old, first_old, second_old, old_owner, new_owner, offsets
):
    devices = old_owner.shape[0]
    row_count, proj_width = weights_old.shape
    tok_rows = hidden.shape[1]
    half_tok = tok_rows // 2
    model_width = hidden.shape[2]
    head_dim = HEAD
    kv_heads = KV_HEADS
    groups = Q_HEADS // KV_HEADS
    key_width = kv_heads * head_dim
    tokens_flat = hidden[0]
    moved = relocate(
        jnp.stack((weights_old, gradient_old, first_old, second_old)), new_owner, old_owner
    )
    weights_new, first_new, second_new = adam_step(moved[0], moved[1], moved[2], moved[3])
    weights_next = adam_step(weights_old, gradient_old, first_old, second_old)[0]
    copies = weights_next.astype(jnp.bfloat16)
    permuted = jnp.take(
        tokens_flat.reshape(tok_rows, devices, row_count), old_owner, axis=1
    ).reshape(tok_rows, model_width)
    segment = lax.all_gather(copies, ("dp", "ctx"), axis=0, tiled=True)
    columns = lax.slice_in_dim(permuted, 0, segment.shape[0], axis=1)
    projected = jnp.zeros((tok_rows, proj_width), jnp.float32) + jnp.dot(
        columns, segment, preferred_element_type=jnp.float32
    )
    offset_table = offsets[0]
    ctx_count = offset_table.shape[0]
    flat_table = offset_table.reshape(2 * ctx_count)
    slot_ids = jnp.arange(2 * ctx_count, dtype=jnp.int32)

    def lookup(rows_global):
        device_of = rows_global // tok_rows
        local_row = rows_global % tok_rows
        slot_index = device_of * 2 + local_row // half_tok
        picked = slot_index[:, None] == slot_ids[None, :]
        return jnp.sum(jnp.where(picked, flat_table[None, :], 0), axis=1) + local_row % half_tok

    own_rows = lax.axis_index("ctx") * tok_rows + jnp.arange(tok_rows, dtype=jnp.int32)
    query_pos = lookup(own_rows)
    key_heads = projected[:, :key_width].reshape(tok_rows, kv_heads, head_dim)
    key_rows = rotate_keys(key_heads, query_pos).reshape(tok_rows, key_width).astype(jnp.bfloat16)
    value_rows = projected[:, key_width:].astype(jnp.bfloat16)
    query_heads = queries[0].reshape(tok_rows, kv_heads, groups, head_dim)
    inv_root = 1.0 / math.sqrt(head_dim)
    best_score = jnp.full((kv_heads, groups, tok_rows), -1e30, jnp.float32)
    key_block = lax.all_gather(key_rows, "ctx", axis=0, tiled=True)
    value_block = lax.all_gather(value_rows, "ctx", axis=0, tiled=True)
    block_rows = key_block.shape[0]
    key_pos = lookup(jnp.arange(block_rows, dtype=jnp.int32))
    key_split = key_block.reshape(block_rows, kv_heads, head_dim)
    scores = (
        jnp.einsum("tkgd,nkd->kgtn", query_heads, key_split, preferred_element_type=jnp.float32)
        * inv_root
    )
    visible = key_pos[None, None, None, :] <= query_pos[None, None, :, None]
    masked = jnp.where(visible, scores, -1e30)
    best_next = jnp.maximum(best_score, jnp.max(masked, axis=3))
    exp_terms = jnp.where(visible, jnp.exp(masked - best_next[..., None]), 0.0)
    totals_next = jnp.sum(exp_terms, axis=3)
    value_split = value_block.reshape(block_rows, kv_heads, head_dim)
    increment = jnp.einsum(
        "kgtn,nkd->tkgd",
        exp_terms.astype(jnp.bfloat16),
        value_split,
        preferred_element_type=jnp.float32,
    )
    result = increment / jnp.transpose(totals_next, (2, 0, 1))[..., None]
    attended = result.reshape(1, tok_rows, Q_HEADS * head_dim).astype(jnp.bfloat16)
    return (weights_new, first_new, second_new, attended)


def solution(mesh):
    in_specs = (
        P("dp", "ctx", None),
        P("dp", "ctx", None),
        P(("dp", "ctx"), None),
        P(("dp", "ctx"), None),
        P(("dp", "ctx"), None),
        P(("dp", "ctx"), None),
        P(),
        P(),
        P("dp", None, None),
    )
    out_specs = (
        P(("dp", "ctx"), None),
        P(("dp", "ctx"), None),
        P(("dp", "ctx"), None),
        P("dp", "ctx", None),
    )
    return jax.shard_map(shards, mesh=mesh, in_specs=in_specs, out_specs=out_specs, check_vma=False)
```

profile of v0, /device:TPU:0, one launch (start us, length us, event | category | flops | bytes accessed | tf_op | source)
XLA Modules:
  0.0 354.3 jit_solution(16640943310294573128)
XLA Ops:
  7.3 3.9 %fusion.19 = bf16[256,1024]{1,0:T(8,128)(2,1)} fusion(f32[256,1024]{1,0:T(8,128)} %param.13, f32[256,1024]{1,0:T(8,128)} %param.14, f32[256,1024]{1,0:T(8,128)} %param.16, f32[256,1024]{1,0:T(8,128)} %param.15), kind=kLoop, calls=%fused_computation.34 | loop fusion | flops 3670016 | bytes 4718592 | tf_op jit(solution)/shard_map/convert_element_type | solution.py:85
  11.1 2.5 copy.55
  13.7 1.3 copy.56
  15.7 3.9 %maximum_bitcast_fusion = f32[32,4,32,256]{3,2,1,0:T(8,128)} fusion(f32[1,256,32,32]{1,3,0,2:T(8,128)S(1)} %bitcast.86, f32[1,256,32,32]{1,3,0,2:T(8,128)S(1)} %bitcast.85, f32[1,256,32,32]{1,3,0,2:T(8,128)} %bitcast.84, f32[1,256,32,32]{1,3,0,2:T(8,128)} %bitcast.83), kind=kLoop, calls=%fused_computation.14 | loop fusion | flops 3145728 | bytes 8388608 | tf_op jit(solution)/shard_map/transpose | solution.py:60
  19.6 5.0 %gather_fusion.1 = f32[32,4,32,256]{3,2,1,0:T(8,128)} fusion(f32[32,4,32,256]{3,2,1,0:T(8,128)} %maximum_bitcast_fusion, s32[1024]{0:T(1024)S(1)} %pad_clamp_fusion.2), kind=kCustom, calls=%fused_computation.clone | custom fusion | bytes 8388736 | tf_op jit(solution)/shard_map/jit(_take)/gather | solution.py:61
  24.6 5.1 %broadcast_select_fusion = f32[32,4,32,256]{3,2,1,0:T(8,128)} fusion(f32[32,4,32,256]{3,2,1,0:T(8,128)} %gather_fusion.1, pred[32]{0:T(512)(128)(4,1)S(1)} %compare_and_fusion.1), kind=kLoop, calls=%fused_computation.18 | loop fusion | flops 1048576 | bytes 8388640 | tf_op jit(solution)/shard_map/jit(_take)/select_n | solution.py:61
  29.7 7.8 %all-to-all-start = ((f32[32,4,32,256]{3,2,1,0:T(8,128)}), f32[32,4,32,256]{3,2,1,0:T(8,128)}, u32[]{:S(2)}, u32[]{:S(2)}) async-start(f32[32,4,32,256]{3,2,1,0:T(8,128)} %broadcast_select_fusion), calls=%async_computation | async-start | bytes 8388608 | tf_op jit(solution)/shard_map/all_to_all | solution.py:62
  37.7 8.6 %copy.67 = bf16[1,384,8192]{1,2,0:T(8,128)(2,1)} copy(bf16[1,384,8192]{2,1,0:T(8,128)(2,1)} %param.11) | data formatting | bytes 12582912 | tf_op args[0]
  46.4 8.6 %copy.68 = bf16[384,32,256]{2,0,1:T(8,128)(2,1)} copy(bf16[384,32,256]{0,2,1:T(8,128)(2,1)} %bitcast.75) | data formatting | bytes 12582912 | tf_op jit(solution)/shard_map/reshape;squeeze | solution.py:87
  55.0 6.4 %gather_fusion = bf16[32,384,256]{2,1,0:T(8,128)(2,1)} fusion(bf16[384,32,256]{2,0,1:T(8,128)(2,1)} %copy.68, s32[1024]{0:T(1024)S(1)} %pad_clamp_fusion), kind=kCustom, calls=%fused_computation.2 | custom fusion | bytes 12583040 | tf_op jit(solution)/shard_map/jit(_take)/gather | solution.py:86
  61.4 8.8 %copy.69 = bf16[384,32,256]{0,2,1:T(8,128)(2,1)} copy(bf16[384,32,256]{2,0,1:T(8,128)(2,1)} %bitcast.74) | data formatting | bytes 12582912 | tf_op jit(solution)/shard_map/jit(_take)/gather | solution.py:86
  70.4 2.5 copy.87
  72.9 0.9 scatter_custom_fusion
  74.1 0.8 multiply_cosine_fusion
  75.2 8.1 %bitcast_select_fusion.1 = bf16[384,8192]{0,1:T(8,128)(2,1)} fusion(bf16[384,32,256]{0,2,1:T(8,128)(2,1)} %copy.69, pred[8192]{0:T(1024)(128)(4,1)S(1)} %broadcast_in_dim.87), kind=kLoop, calls=%fused_computation.13 | loop fusion | flops 3145728 | bytes 12591104 | tf_op jit(solution)/shard_map/jit(_take)/select_n | solution.py:86
  83.3 112.0 %all-to-all-done = f32[32,4,32,256]{3,2,1,0:T(8,128)} async-done(((f32[32,4,32,256]{3,2,1,0:T(8,128)}), f32[32,4,32,256]{3,2,1,0:T(8,128)}, u32[]{:S(2)}, u32[]{:S(2)}) %all-to-all-start) | async-done | bytes 4194336 | tf_op jit(solution)/shard_map/all_to_all | solution.py:62
  195.3 5.3 %gather_fusion.2 = f32[32,4,32,256]{3,2,1,0:T(8,128)} fusion(f32[32,4,32,256]{3,2,1,0:T(8,128)} %all-to-all-done, s32[1024]{0:T(1024)S(1)} %pad_clamp_fusion.1), kind=kCustom, calls=%fused_computation.1.clone | custom fusion | bytes 8388736 | tf_op jit(solution)/shard_map/jit(_take)/gather | solution.py:63
  200.6 12.1 %fusion.54 = f32[384,1024]{1,0:T(8,128)S(1)} fusion(bf16[384,8192]{0,1:T(8,128)(2,1)} %bitcast_select_fusion.1, bf16[8192,1024]{1,0:T(8,128)(2,1)} %all-gather.4.cloned.1.call-done), kind=kOutput, calls=%fused_computation.102 | convolution fusion | flops 6442450944 | bytes 24641536 | tf_op jit(solution)/shard_map/dot_general | solution.py:91
  212.7 1.0 slice.48
  213.7 1.4 reshape.259
  215.1 0.6 subtract_convert_fusion
  216.2 1.0 copy.71
  217.3 2.7 select_bitcast_fusion
  220.0 0.8 slice_multiply_fusion.1
  221.1 2.0 multiply_subtract_fusion
  223.2 0.8 slice.58
  224.0 31.4 %all-gather.8.cloned.1.call-done = bf16[1536,512]{0,1:T(8,128)(2,1)} async-done(((bf16[384,512]{0,1:T(8,128)(2,1)}), bf16[1536,512]{0,1:T(8,128)(2,1)}) %all-gather.8.cloned.1.call-update) | async-done | bytes 1572880 | tf_op jit(solution)/shard_map/all_gather | solution.py:114
  255.4 30.2 %fusion = (f32[4,8,384]{2,1,0:T(8,128)S(1)}, f32[4,1536,384,8]{2,1,3,0:T(8,128)}) fusion(pred[384,1536]{0,1:T(8,128)(4,1)S(1)} %broadcast_compare_fusion, bf16[1536,4,128,1]{0,2,3,1:T(8,128)(2,1)} %bitcast.91, bf16[384,4,8,128]{3,2,1,0:T(8,128)(2,1)} %bitcast.76), kind=kOutput, calls=%fused_computation.6 | convolution fusion | flops 4888449024 | bytes 80855040 | tf_op jit(solution)/shard_map/tkgd,nkd->kgtn/dot_general | solution.py:120
  285.6 24.2 %fusion.1 = f32[4,8,384]{2,1,0:T(8,128)S(1)} fusion(f32[4,1536,384,8]{2,1,3,0:T(8,128)} %get-tuple-element.35, f32[4,8,384]{2,1,0:T(8,128)S(1)} %broadcast_maximum_fusion, pred[384,1536]{0,1:T(8,128)(4,1)S(1)} %broadcast_compare_fusion), kind=kLoop, calls=%fused_computation.7 | loop fusion | flops 94359552 | bytes 76185600 | tf_op jit(solution)/shard_map/reduce_sum | solution.py:127
  309.8 1.7 copy.80
  311.5 31.6 %fusion.6 = bf16[384,4,8,128]{0,3,2,1:T(8,128)(2,1)} fusion(f32[384,4,8]{0,2,1:T(8,128)S(1)} %bitcast.94, bf16[1536,4,128,1]{0,2,3,1:T(8,128)(2,1)S(1)} %bitcast.92, f32[4,1536,384,8]{2,1,3,0:T(8,128)} %get-tuple-element.35, f32[4,8,384]{2,1,0:T(8,128)S(1)} %broadcast_maximum_fusion, pred[384,1536]{0,1:T(8,128)(4,1)S(1)} %broadcast_compare_fusion), kind=kOutput, calls=%fused_computation.12 | convolution fusion | flops 4929355776 | bytes 80904192 | tf_op jit(solution)/shard_map/kgtn,nkd->tkgd/dot_general | solution.py:129
  343.1 4.6 %copy.76 = bf16[1,384,4096]{2,1,0:T(8,128)(2,1)} copy(bf16[1,384,4096]{1,2,0:T(8,128)(2,1)} %bitcast.90) | data formatting | bytes 6291456
  (52 shorter events, 2.7 us)
Async XLA Ops:
  7.2 6.5 %copy-start = (f32[256,1024]{1,0:T(8,128)S(1)}, f32[256,1024]{1,0:T(8,128)}, u32[]{:S(2)}) copy-start(f32[256,1024]{1,0:T(8,128)} %param.14) | copy-start | bytes 3145732
  7.2 7.8 %copy-start.1 = (f32[256,1024]{1,0:T(8,128)S(1)}, f32[256,1024]{1,0:T(8,128)}, u32[]{:S(2)}) copy-start(f32[256,1024]{1,0:T(8,128)} %param.15) | copy-start | bytes 3145732
  7.2 8.1 %copy-start.2 = (f32[256,1024]{1,0:T(8,128)S(1)}, f32[256,1024]{1,0:T(8,128)}, u32[]{:S(2)}) copy-start(f32[256,1024]{1,0:T(8,128)} %param.16) | copy-start | bytes 3145732
  7.2 8.5 %copy-start.5 = (s32[32]{0:T(128)S(1)}, s32[32]{0:T(128)}, u32[]{:S(2)}) copy-start(s32[32]{0:T(128)} %param.18) | copy-start | bytes 388
  7.2 193.4 %all-gather.4.cloned.1.call-start = ((), (), s32[]{:S(2)}) async-start(), calls=%async_computation.1 | async-start | bytes 17301504 | tf_op jit(solution)/shard_map/all_gather | solution.py:89
  29.7 7.8 %copy-start.4 = (s32[1,4,2]{1,2,0:T(2,128)S(1)}, s32[1,4,2]{1,2,0:T(2,128)}, u32[]{:S(2)}) copy-start(s32[1,4,2]{1,2,0:T(2,128)} %param.19) | copy-start | bytes 100
  29.7 165.6 %all-to-all-start = ((f32[32,4,32,256]{3,2,1,0:T(8,128)}), f32[32,4,32,256]{3,2,1,0:T(8,128)}, u32[]{:S(2)}, u32[]{:S(2)}) async-start(f32[32,4,32,256]{3,2,1,0:T(8,128)} %broadcast_select_fusion), calls=%async_computation | async-start | bytes 8388608 | tf_op jit(solution)/shard_map/all_to_all | solution.py:62
  37.5 217.9 %all-gather.8.cloned.1.call-start = ((), (), s32[]{:S(2)}) async-start(), calls=%async_computation.3 | async-start | bytes 1966080 | tf_op jit(solution)/shard_map/all_gather | solution.py:114
  46.4 8.6 %copy-start.6 = (s32[32]{0:T(128)S(1)}, s32[32]{0:T(128)}, u32[]{:S(2)}) copy-start(s32[32]{0:T(128)} %param.17) | copy-start | bytes 388
  61.4 8.9 %copy-start.3 = (bf16[1,384,4096]{2,1,0:T(8,128)(2,1)S(1)}, bf16[1,384,4096]{2,1,0:T(8,128)(2,1)}, u32[]{:S(2)}) copy-start(bf16[1,384,4096]{2,1,0:T(8,128)(2,1)} %param.12) | copy-start | bytes 9437188
  217.3 92.5 %all-gather.6.cloned.1.call-start = ((), (), s32[]{:S(2)}) async-start(), calls=%async_computation.2 | async-start | bytes 1966080 | tf_op jit(solution)/shard_map/all_gather | solution.py:115
Sparse Core Ops, SparseCore 0:
  11.6 186.3 all-gather.3
  217.4 37.9 all-gather.7
  257.0 36.0 all-gather.5
where the time goes:
time: 355 us; the launch traced here: 354 us
  waiting for transfers between devices  144 us (41%)
  matrix products  73.9 us (21%)
  local copies, waits for them, and re-layouts  61.8 us (17%)
  other arithmetic  53.2 us (15%)
  between operations  14 us (4%)
  starting transfers between devices  7.88 us (2%)
    all_to_all x1, waiting for transfers between devices, relocate(): lax.all_to_all(outgoing, ('dp', 'ctx'), split_axis=0, concat_axis=0, tile...  112 us
    dot_general x1, matrix products, shards(): jnp.einsum('kgtn,nkd->tkgd', exp_terms.astype(jnp.bfloat16), value_split,...  31.6 us
    all_gather x1, waiting for transfers between devices, shards(): key_block = lax.all_gather(key_rows, 'ctx', axis=0, tiled=True)  31.4 us
    dot_general x1, matrix products, shards(): jnp.einsum('tkgd,nkd->kgtn', query_heads, key_split, preferred_element_ty...  30.2 us
    reduce_sum x1, other arithmetic, shards(): totals_next = jnp.sum(exp_terms, axis=3)  24.2 us
    unnamed x26, local copies, waits for them, and re-layouts  20.7 us
    gather x2, local copies, waits for them, and re-layouts, shards(): jnp.take(tokens_flat.reshape(tok_rows, devices, row_count), old_owner, ax...  15.2 us
    dot_general x1, matrix products, shards(): jnp.dot(columns, segment, preferred_element_type=jnp.float32)  12.1 us
  transfers between devices with their start and end apart: 4, of which 2 were waited for; matrix products, arithmetic and copies ran while one was open for 37% of the time, Pallas kernels for 0%

commit v1 on v0

v1 whole, which is shorter than its diff:
```python
import functools
import math

import jax
import jax.numpy as jnp
from jax import lax
from jax.experimental import pallas as pl
from jax.experimental.pallas import tpu as pltpu
from jax.sharding import PartitionSpec as P

HEAD = 128
KV_HEADS = 4
Q_HEADS = 32
GROUPS = Q_HEADS // KV_HEADS
CHUNKS = 2
LANES = 128
VMEM_LIMIT = 48 * 1024 * 1024

learn_rate = 0.0003
beta_one = 0.9
beta_two = 0.95
adam_eps = 1e-08
decay_rate = 0.1
step_number = 1000
corr_one = 1.0 - beta_one**step_number
corr_two = 1.0 - beta_two**step_number
rope_base = 500000.0


def moments(gradient, first_mom, second_mom):
    first_next = beta_one * first_mom + (1.0 - beta_one) * gradient
    second_next = beta_two * second_mom + (1.0 - beta_two) * gradient * gradient
    return first_next, second_next


def update(weights, first_next, second_next):
    direction = first_next / corr_one / (jnp.sqrt(second_next / corr_two) + adam_eps)
    return weights - learn_rate * (direction + decay_rate * weights)


def invert(owners):
    ids = jnp.arange(owners.shape[0], dtype=jnp.int32)
    return jnp.sum(jnp.where(owners[None, :] == ids[:, None], ids[None, :], 0), axis=1)


def moments_kernel(new_owner, g_ref, m_ref, v_ref, out_ref, first_t, second_t):
    first_next, second_next = moments(g_ref[...], m_ref[...], v_ref[...])
    first_t[...] = first_next.T
    second_t[...] = second_next.T
    devices, both, _ = out_ref.shape
    cols = both // 2

    def body(dest, carry):
        rows = pl.ds(pl.multiple_of(new_owner[dest] * cols, cols), cols)
        out_ref[dest] = jnp.concatenate([first_t[rows], second_t[rows]], axis=0).astype(out_ref.dtype)
        return carry

    lax.fori_loop(0, devices, body, 0)


def outgoing_moments(new_owner, gradient, first_mom, second_mom):
    rows, width = gradient.shape
    devices = new_owner.shape[0]
    whole = pl.BlockSpec(memory_space=pltpu.VMEM)
    return pl.pallas_call(
        moments_kernel,
        out_shape=jax.ShapeDtypeStruct((devices, 2 * width // devices, rows), jnp.bfloat16),
        in_specs=[pl.BlockSpec(memory_space=pltpu.SMEM), whole, whole, whole],
        out_specs=whole,
        scratch_shapes=[pltpu.VMEM((width, rows), jnp.float32)] * 2,
        compiler_params=pltpu.CompilerParams(vmem_limit_bytes=VMEM_LIMIT),
        cost_estimate=pl.CostEstimate(flops=10 * rows * width, bytes_accessed=16 * rows * width, transcendentals=0),
        name="moments",
    )(new_owner, gradient, first_mom, second_mom)


def order_kernel(inverse, in_ref, first_ref, second_ref):
    devices, both, rows = in_ref.shape
    cols = both // 2
    for block in range(devices):
        value = in_ref[inverse[block]].astype(jnp.float32)
        first_ref[:, block * rows : (block + 1) * rows] = value[:cols]
        second_ref[:, block * rows : (block + 1) * rows] = value[cols:]


def ordered_moments(inverse, incoming):
    devices, both, rows = incoming.shape
    whole = pl.BlockSpec(memory_space=pltpu.VMEM)
    shape = jax.ShapeDtypeStruct((both // 2, devices * rows), jnp.float32)
    return pl.pallas_call(
        order_kernel,
        out_shape=(shape, shape),
        in_specs=[pl.BlockSpec(memory_space=pltpu.SMEM), whole],
        out_specs=(whole, whole),
        compiler_params=pltpu.CompilerParams(vmem_limit_bytes=VMEM_LIMIT),
        cost_estimate=pl.CostEstimate(flops=0, bytes_accessed=6 * devices * both * rows, transcendentals=0),
        name="order",
    )(inverse, incoming)


def project_kernel(parts, inverse, feature, hidden_ref, cos_ref, sin_ref, *refs):
    w_refs, new_ref, outs, total = refs[:parts], refs[parts], refs[parts + 1 : -1], refs[-1]
    step = pl.program_id(0)
    block = jnp.concatenate([w[...] for w in w_refs], axis=0)
    term = jnp.dot(hidden_ref[...], block, preferred_element_type=jnp.float32)

    @pl.when(step == 0)
    def _():
        total[...] = term

    @pl.when(step > 0)
    def _():
        total[...] += term

    cols = new_ref.shape[0]
    first = feature[0] * cols
    base = pl.multiple_of(first // LANES * LANES, LANES)
    lanes = jnp.concatenate([w[:, pl.ds(base, LANES)] for w in w_refs], axis=0)
    here = lax.broadcasted_iota(jnp.int32, (cols, LANES), 1)
    want = lax.broadcasted_iota(jnp.int32, (cols, LANES), 0) + (first - base)
    pick = (here == want).astype(jnp.float32).astype(jnp.bfloat16)
    new_ref[...] = lax.dot_general(pick, lanes, (((1,), (1,)), ((), ())), preferred_element_type=jnp.float32)

    @pl.when(step == pl.num_programs(0) - 1)
    def _():
        cosine, sine = cos_ref[...], sin_ref[...]
        per = KV_HEADS // len(outs)
        for head in range(KV_HEADS):
            key = total[:, head * HEAD : (head + 1) * HEAD]
            turned = jnp.concatenate([key[:, HEAD // 2 :], key[:, : HEAD // 2]], axis=1)
            value = total[:, (KV_HEADS + head) * HEAD : (KV_HEADS + head + 1) * HEAD]
            out, at = outs[head // per], head % per * 2 * HEAD
            out[:, at : at + HEAD] = (key * cosine + turned * sine).astype(jnp.bfloat16)
            out[:, at + HEAD : at + 2 * HEAD] = value.astype(jnp.bfloat16)


def project(inverse, feature, hidden, cosine, sine, gathered):
    _, tokens, depth = hidden.shape
    devices = inverse.shape[0]
    rows, width = depth // devices, gathered.shape[1]
    parts = min(devices, max(1, 1024 // rows))
    wide = parts * rows
    cols = width // devices

    def weight_spec(part):
        return pl.BlockSpec((rows, width), lambda i, inv, feat: (inv[i * parts + part], 0))

    table = pl.BlockSpec((tokens, HEAD), lambda i, inv, feat: (0, 0))
    out_width = 2 * HEAD * KV_HEADS // CHUNKS
    return pl.pallas_call(
        functools.partial(project_kernel, parts),
        out_shape=[jax.ShapeDtypeStruct((cols, depth), jnp.float32)]
        + [jax.ShapeDtypeStruct((tokens, out_width), jnp.bfloat16)] * CHUNKS,
        grid_spec=pltpu.PrefetchScalarGridSpec(
            num_scalar_prefetch=2,
            grid=(depth // wide,),
            in_specs=[pl.BlockSpec((None, tokens, wide), lambda i, inv, feat: (0, 0, i)), table, table]
            + [weight_spec(part) for part in range(parts)],
            out_specs=[pl.BlockSpec((cols, wide), lambda i, inv, feat: (0, i))]
            + [pl.BlockSpec((tokens, out_width), lambda i, inv, feat: (0, 0))] * CHUNKS,
            scratch_shapes=[pltpu.VMEM((tokens, width), jnp.float32)],
        ),
        compiler_params=pltpu.CompilerParams(vmem_limit_bytes=VMEM_LIMIT),
        cost_estimate=pl.CostEstimate(
            flops=2 * tokens * depth * width, bytes_accessed=2 * depth * (tokens + width), transcendentals=0
        ),
        name="project",
    )(inverse, feature, hidden, cosine, sine, *([gathered] * parts))


def attend_kernel(chunk, slots, own, q_ref, kv_ref, *refs):
    out_ref, keys, values = refs[-3:]
    half = q_ref.shape[0]
    seq = kv_ref.shape[0]
    wide = 2 * half
    segment = pl.program_id(1)

    @pl.when(segment == 0)
    def _():
        for place in range(seq // half):
            rows = pl.ds(pl.multiple_of(slots[place] * half, half), half)
            keys[place * half : (place + 1) * half] = kv_ref[rows, :HEAD]
            values[place * half : (place + 1) * half] = kv_ref[rows, HEAD:]

    index = own[segment]
    scale = math.log2(math.e) / math.sqrt(HEAD)

    def one_head(head, blocks, visible):
        at = pl.ds(pl.multiple_of(head * HEAD, HEAD), HEAD)
        query = q_ref[:, at]
        scores = []
        for block in range(blocks):
            score = lax.dot_general(
                query,
                keys[block * wide : (block + 1) * wide],
                (((1,), (1,)), ((), ())),
                preferred_element_type=jnp.float32,
            )
            scores.append(jnp.where(visible, score, -1e30) if block == blocks - 1 else score)
        best = jnp.max(functools.reduce(jnp.maximum, scores), axis=1, keepdims=True)
        weights = [jnp.exp2((score - best) * scale) for score in scores]
        summed = jnp.sum(functools.reduce(jnp.add, weights), axis=1, keepdims=True)
        result = functools.reduce(
            jnp.add,
            [
                jnp.dot(
                    weight.astype(jnp.bfloat16),
                    values[block * wide : (block + 1) * wide],
                    preferred_element_type=jnp.float32,
                )
                for block, weight in enumerate(weights)
            ],
        )
        out_ref[:, at] = (result / summed).astype(jnp.bfloat16)

    for blocks in range(1, seq // wide + 1):

        @pl.when(index // 2 + 1 == blocks)
        def _():
            row = lax.broadcasted_iota(jnp.int32, (half, wide), 0)
            visible = lax.broadcasted_iota(jnp.int32, (half, wide), 1) <= row + index % 2 * half

            def body(pair, carry):
                for head in range(2):
                    one_head(pair * 2 + head, blocks, visible)
                return carry

            lax.fori_loop(0, GROUPS // 2, body, 0)


def attend(chunk, slots, own, queries, gathered, earlier):
    _, tokens, width = queries.shape
    seq = gathered.shape[0]
    half = tokens // 2
    per = KV_HEADS // CHUNKS
    spec = pl.BlockSpec((None, half, GROUPS * HEAD), lambda g, s, slots, own: (0, s, chunk * per + g))
    more, specs, aliases = (), [], {}
    if earlier is not None:
        more, specs, aliases = (earlier,), [pl.BlockSpec(memory_space=pl.ANY)], {4: 0}
    return pl.pallas_call(
        functools.partial(attend_kernel, chunk),
        out_shape=jax.ShapeDtypeStruct(queries.shape, jnp.bfloat16),
        grid_spec=pltpu.PrefetchScalarGridSpec(
            num_scalar_prefetch=2,
            grid=(per, 2),
            in_specs=[spec, pl.BlockSpec((seq, 2 * HEAD), lambda g, s, slots, own: (0, g))] + specs,
            out_specs=spec,
            scratch_shapes=[pltpu.VMEM((seq, HEAD), jnp.bfloat16)] * 2,
        ),
        input_output_aliases=aliases,
        compiler_params=pltpu.CompilerParams(vmem_limit_bytes=VMEM_LIMIT),
        cost_estimate=pl.CostEstimate(
            flops=4 * tokens * seq * width // CHUNKS,
            bytes_accessed=4 * tokens * width // CHUNKS,
            transcendentals=tokens * seq * width // HEAD // CHUNKS // 2,
        ),
        name=f"attend{chunk}",
    )(slots, own, queries, gathered, *more)


def shards(
    hidden, queries, weights_old, gradient_old, first_old, second_old, old_owner, new_owner, offsets
):
    both = ("dp", "ctx")
    tokens = hidden.shape[1]
    half = tokens // 2
    first_next, second_next = moments(gradient_old, first_old, second_old)
    copies = update(weights_old, first_next, second_next).astype(jnp.bfloat16)
    gathered = lax.all_gather(copies, both, axis=0, tiled=True)
    outgoing = outgoing_moments(new_owner, gradient_old, first_old, second_old)
    incoming = lax.all_to_all(outgoing, both, split_axis=0, concat_axis=0, tiled=True)

    inverse = invert(old_owner)
    device = lax.axis_index(both)
    feature = lax.dynamic_slice(new_owner, (device,), (1,))
    starts = offsets[0] // half
    slots = invert(starts.reshape(-1))
    own = lax.dynamic_slice(starts, (lax.axis_index("ctx"), 0), (1, 2)).reshape(2)

    positions = (own[:, None] * half + jnp.arange(half, dtype=jnp.int32)[None, :]).reshape(tokens)
    exponent = jnp.arange(HEAD // 2, dtype=jnp.float32) * (2.0 / HEAD)
    inv_freq = jnp.power(rope_base, -exponent)
    angles = positions.astype(jnp.float32)[:, None] * inv_freq
    cosine, sine = jnp.cos(angles), jnp.sin(angles)
    cosine = jnp.concatenate([cosine, cosine], axis=1)
    sine = jnp.concatenate([-sine, sine], axis=1)

    weights_new, *chunks = project(inverse, feature, hidden, cosine, sine, gathered)
    whole = [lax.all_gather(chunk, "ctx", axis=0, tiled=True) for chunk in chunks]
    first_new, second_new = ordered_moments(inverse, incoming)
    attended = None
    for chunk in range(CHUNKS):
        attended = attend(chunk, slots, own, queries, whole[chunk], attended)
    return (weights_new, first_new, second_new, attended)


def solution(mesh):
    states = P(("dp", "ctx"), None)
    tokens = P("dp", "ctx", None)
    in_specs = (tokens, tokens, states, states, states, states, P(), P(), P("dp", None, None))
    out_specs = (states, states, states, tokens)
    return jax.shard_map(shards, mesh=mesh, in_specs=in_specs, out_specs=out_specs, check_vma=False)
```

time: 355 us -> 269 us (0.76)
  matrix products: 73.9 us -> 0 us
  Pallas kernels: 0 us -> 58.8 us
  local copies, waits for them, and re-layouts: 61.8 us -> 6.99 us
  other arithmetic: 53.2 us -> 5.01 us
  waiting for transfers between devices: 144 us -> 181 us
  starting transfers between devices: 7.88 us -> 2.89 us
    all_gather x3, waiting for transfers between devices: 31.4 us -> 134 us  [the longest x1 116 us: shards(): gathered = lax.all_gather(copies, both, axis=0, tiled=True)]
    dot_general x3 -> x0, matrix products: 73.9 us -> none  [the longest x1 31.6 us: shards(): jnp.einsum('kgtn,nkd->tkgd', exp_terms.astype(jnp.bfloat16), value_split,...]
    all_to_all x1, waiting for transfers between devices: 112 us -> 45.9 us  [shards(): lax.all_to_all(outgoing, both, split_axis=0, concat_axis=0, tiled=True)]
    pallas_call x0 -> x5, Pallas kernels: none -> 58.8 us  [the longest x2 37.9 us: attend(): pl.pallas_call(functools.partial(attend_kernel, chunk), out_shape=jax.Sha...]
    gather x4 -> x0, local copies, waits for them, and re-layouts: 25.5 us -> none  [the longest x2 15.2 us: shards(): jnp.take(tokens_flat.reshape(tok_rows, devices, row_count), old_owner, ax...]
    reduce_sum x3 -> x2, other arithmetic: 24.4 us -> 0.23 us  [invert(): jnp.sum(jnp.where(owners[None, :] == ids[:, None], ids[None, :], 0), axis=1)]
    unnamed x26, local copies, waits for them, and re-layouts: 20.7 us -> 5.85 us
    select_n x5 -> x2, other arithmetic: 13.1 us -> 0.01 us  [shards(): starts = offsets[0] // half]
  transfers between devices with their start and end apart: 4 -> 4, of which waited for: 2 -> 4; matrix products, arithmetic and copies ran while one was open for 37% -> 1% of each run, Pallas kernels for 0% -> 9%
where the time goes in v1:
time: 269 us; the launch traced here: 268 us
  waiting for transfers between devices  181 us (67%)
  Pallas kernels  58.8 us (22%)
  between operations  13.9 us (5%)
  local copies, waits for them, and re-layouts  6.99 us (3%)
  other arithmetic  5.01 us (2%)
  starting transfers between devices  2.89 us (1%)
    all_gather x1, waiting for transfers between devices, shards(): gathered = lax.all_gather(copies, both, axis=0, tiled=True)  116 us
    all_to_all x1, waiting for transfers between devices, shards(): lax.all_to_all(outgoing, both, split_axis=0, concat_axis=0, tiled=True)  45.9 us
    pallas_call x2, Pallas kernels, attend(): pl.pallas_call(functools.partial(attend_kernel, chunk), out_shape=jax.Sha...  37.9 us
    all_gather x2, waiting for transfers between devices, shards(): lax.all_gather(chunk, 'ctx', axis=0, tiled=True)  18.3 us
    pallas_call x1, Pallas kernels, project(): pl.pallas_call(functools.partial(project_kernel, parts), out_shape=[jax.S...  16.5 us
    unnamed x26, local copies, waits for them, and re-layouts  5.85 us
  transfers between devices with their start and end apart: 4, of which 4 were waited for; matrix products, arithmetic and copies ran while one was open for 1% of the time, Pallas kernels for 9%

profile of v1, /device:TPU:0, one launch (start us, length us, event | category | flops | bytes accessed | tf_op | source)
XLA Modules:
  0.0 268.3 jit_solution(6216977056536428768)
XLA Ops:
  7.2 0.0 all-gather.4.cloned.1.call-start
  7.2 3.7 %fusion.7 = bf16[256,1024]{1,0:T(8,128)(2,1)} fusion(f32[256,1024]{1,0:T(8,128)} %param.11, f32[256,1024]{1,0:T(8,128)} %g_ref.1, f32[256,1024]{1,0:T(8,128)} %v_ref.1, f32[256,1024]{1,0:T(8,128)} %m_ref.1), kind=kLoop, calls=%fused_computation.8 | loop fusion | flops 3670016 | bytes 4718592 | tf_op jit(solution)/shard_map/convert_element_type | solution.py:268
  11.0 0.0 all-gather.8.cloned.1.call-start
  11.1 0.1 copy.24
  11.2 0.1 copy.25
  11.3 0.4 copy-done.10
  11.7 0.1 add_convert_fusion
  11.7 0.1 convert_element_type.14
  11.8 0.6 dynamic_slice.6.feature
  12.4 0.1 select_reduce_fusion.inverse
  12.5 0.8 fusion.8
  13.3 0.2 pad_maximum_fusion
  13.5 115.7 %all-gather.4.cloned.1.call-done.refs_0_.refs_1_.refs_2_.refs_3_ = bf16[8192,1024]{1,0:T(8,128)(2,1)} async-done(((bf16[256,1024]{1,0:T(8,128)(2,1)}), bf16[8192,1024]{1,0:T(8,128)(2,1)}) %all-gather.4.cloned.1.call-update) | async-done | bytes 16777232 | tf_op jit(solution)/shard_map/all_gather | solution.py:269
  129.2 16.5 %project.1 = (f32[32,8192]{1,0:T(8,128)}, bf16[384,512]{1,0:T(8,128)(2,1)S(1)}, bf16[384,512]{1,0:T(8,128)(2,1)}) custom-call(s32[32]{0:T(128)S(1)} %select_reduce_fusion.inverse, s32[1]{0:T(128)} %dynamic_slice.6.feature, bf16[1,384,8192]{2,1,0:T(8,128)(2,1)} %hidden_ref.1, f32[384,128]{1,0:T(8,128)S(1)} %get-tuple-element.19.cos_ref, ...), custom_call_target="tpu_custom_call" | custom-call | flops 6442450944 | bytes 23068672 | tf_op jit(solution)/shard_map/project/pallas_call | solution.py:150
  145.7 0.7 copy-done.3
  146.6 2.4 moments.1
  149.0 2.8 %all-to-all-start = ((bf16[32,64,256]{2,1,0:T(8,128)(2,1)}), bf16[32,64,256]{2,1,0:T(8,128)(2,1)S(1)}, u32[]{:S(2)}, u32[]{:S(2)}) async-start(bf16[32,64,256]{2,1,0:T(8,128)(2,1)} %moments.1), calls=%async_computation | async-start | bytes 2097152 | tf_op jit(solution)/shard_map/all_to_all | solution.py:271
  151.8 0.0 all-gather.6.cloned.1.call-start
  151.8 0.7 all-gather.6.cloned.1.call-update
  152.5 0.1 and.18
  152.6 0.1 copy.28
  152.7 0.1 div.24
  152.8 0.1 select_reduce_fusion.1.slots
  152.9 45.9 %all-to-all-done.in_ref = bf16[32,64,256]{2,1,0:T(8,128)(2,1)S(1)} async-done(((bf16[32,64,256]{2,1,0:T(8,128)(2,1)}), bf16[32,64,256]{2,1,0:T(8,128)(2,1)S(1)}, u32[]{:S(2)}, u32[]{:S(2)}) %all-to-all-start) | async-done | bytes 1048608 | tf_op jit(solution)/shard_map/all_to_all | solution.py:271
  198.8 2.0 order.1
  200.8 2.8 %all-gather.8.cloned.1.call-done.kv_ref = bf16[1536,512]{1,0:T(8,128)(2,1)} async-done(((bf16[384,512]{1,0:T(8,128)(2,1)}), bf16[1536,512]{1,0:T(8,128)(2,1)}) %all-gather.8.cloned.1.call-update) | async-done | bytes 1572880 | tf_op jit(solution)/shard_map/all_gather | solution.py:289
  203.7 1.9 copy-done.5
  205.5 1.4 copy-done.7
  207.0 18.9 %attend0.1.refs_0_ = bf16[1,384,4096]{2,1,0:T(8,128)(2,1)} custom-call(s32[8]{0:T(128)S(1)} %select_reduce_fusion.1.slots, s32[2]{0:T(128)S(1)} %get-tuple-element.15.own, bf16[1,384,4096]{2,1,0:T(8,128)(2,1)S(1)} %copy-done.5, bf16[1536,512]{1,0:T(8,128)(2,1)S(1)} %copy-done.7), custom_call_target="tpu_custom_call" | custom-call | flops 4831838208 | bytes 3145728 | tf_op jit(solution)/shard_map/attend0/pallas_call | solution.py:240
  225.9 15.5 %all-gather.6.cloned.1.call-done.kv_ref = bf16[1536,512]{1,0:T(8,128)(2,1)} async-done(((bf16[384,512]{1,0:T(8,128)(2,1)}), bf16[1536,512]{1,0:T(8,128)(2,1)}) %all-gather.6.cloned.1.call-update) | async-done | bytes 1572880 | tf_op jit(solution)/shard_map/all_gather | solution.py:289
  241.4 1.4 copy-done.8
  242.8 19.0 %attend1.1 = bf16[1,384,4096]{2,1,0:T(8,128)(2,1)} custom-call(s32[8]{0:T(128)S(1)} %select_reduce_fusion.1.slots, s32[2]{0:T(128)S(1)} %get-tuple-element.15.own, bf16[1,384,4096]{2,1,0:T(8,128)(2,1)S(1)} %copy-done.6, bf16[1536,512]{1,0:T(8,128)(2,1)S(1)} %copy-done.8, bf16[1,384,4096]{2,1,0:T(8,128)(2,1)} %attend0.1.refs_0_), custom_call_target="tpu_custom_call", output_to_operand_aliasing={{}: (4, {})} | custom-call | flops 4831838208 | bytes 3145728 | tf_op jit(solution)/shard_map/attend1/pallas_call | solution.py:240
  (30 shorter events, 0.1 us)
Async XLA Ops:
  7.2 3.9 %copy-start.9 = (s32[1,4,2]{1,2,0:T(2,128)S(1)}, s32[1,4,2]{1,2,0:T(2,128)}, u32[]{:S(2)}) copy-start(s32[1,4,2]{1,2,0:T(2,128)} %param.17) | copy-start | bytes 100
  7.2 4.6 %copy-start.4 = (s32[32]{0:T(128)S(1)}, s32[32]{0:T(128)}, u32[]{:S(2)}) copy-start(s32[32]{0:T(128)} %new_owner.1) | copy-start | bytes 388
  7.2 5.2 %copy-start.12 = (s32[32]{0:T(128)S(1)}, s32[32]{0:T(128)}, u32[]{:S(2)}) copy-start(s32[32]{0:T(128)} %param.15) | copy-start | bytes 388
  7.2 122.0 %all-gather.4.cloned.1.call-start = ((), (), s32[]{:S(2)}) async-start(), calls=%async_computation.1 | async-start | bytes 17301504 | tf_op jit(solution)/shard_map/all_gather | solution.py:269
  11.0 192.7 %all-gather.8.cloned.1.call-start = ((), (), s32[]{:S(2)}) async-start(), calls=%async_computation.3 | async-start | bytes 1966080 | tf_op jit(solution)/shard_map/all_gather | solution.py:289
  11.2 0.5 copy-start.10
  129.2 17.3 %copy-start = (f32[256,1024]{1,0:T(8,128)S(1)}, f32[256,1024]{1,0:T(8,128)}, u32[]{:S(2)}) copy-start(f32[256,1024]{1,0:T(8,128)} %g_ref.1) | copy-start | bytes 3145732
  129.2 17.3 %copy-start.1 = (f32[256,1024]{1,0:T(8,128)S(1)}, f32[256,1024]{1,0:T(8,128)}, u32[]{:S(2)}) copy-start(f32[256,1024]{1,0:T(8,128)} %v_ref.1) | copy-start | bytes 3145732
  129.2 17.3 %copy-start.2 = (f32[256,1024]{1,0:T(8,128)S(1)}, f32[256,1024]{1,0:T(8,128)}, u32[]{:S(2)}) copy-start(f32[256,1024]{1,0:T(8,128)} %m_ref.1) | copy-start | bytes 3145732
  145.7 0.7 copy-start.3
  146.5 6.0 %copy-start.11 = (pred[1,4,2]{2,1,0:T(4,128)(4,1)S(1)}, pred[1,4,2]{2,1,0:T(4,128)(4,1)}, u32[]{:S(2)}) copy-start(pred[1,4,2]{2,1,0:T(4,128)(4,1)} %copy-done.10) | copy-start | bytes 28
  149.0 49.9 %all-to-all-start = ((bf16[32,64,256]{2,1,0:T(8,128)(2,1)}), bf16[32,64,256]{2,1,0:T(8,128)(2,1)S(1)}, u32[]{:S(2)}, u32[]{:S(2)}) async-start(bf16[32,64,256]{2,1,0:T(8,128)(2,1)} %moments.1), calls=%async_computation | async-start | bytes 2097152 | tf_op jit(solution)/shard_map/all_to_all | solution.py:271
  151.8 89.7 %all-gather.6.cloned.1.call-start = ((), (), s32[]{:S(2)}) async-start(), calls=%async_computation.2 | async-start | bytes 1966080 | tf_op jit(solution)/shard_map/all_gather | solution.py:289
  203.7 1.9 copy-start.5
  205.5 1.4 copy-start.7
  207.0 34.5 %copy-start.6 = (bf16[1,384,4096]{2,1,0:T(8,128)(2,1)S(1)}, bf16[1,384,4096]{2,1,0:T(8,128)(2,1)}, u32[]{:S(2)}) copy-start(bf16[1,384,4096]{2,1,0:T(8,128)(2,1)} %q_ref.3) | copy-start | bytes 9437188
  241.4 1.4 copy-start.8
Sparse Core Ops, SparseCore 0:
  11.6 117.5 all-gather.3
  146.6 56.9 all-gather.7
  205.2 36.1 all-gather.5

commit v2 on v1

--- a/solution.py
+++ b/solution.py
@@ -12,7 +12,7 @@
 KV_HEADS = 4
 Q_HEADS = 32
 GROUPS = Q_HEADS // KV_HEADS
-CHUNKS = 2
+CHUNKS = 1
 LANES = 128
 VMEM_LIMIT = 48 * 1024 * 1024
 
@@ -138,7 +138,7 @@
     _, tokens, depth = hidden.shape
     devices = inverse.shape[0]
     rows, width = depth // devices, gathered.shape[1]
-    parts = min(devices, max(1, 1024 // rows))
+    parts = min(devices, max(1, 2048 // rows))
     wide = parts * rows
     cols = width // devices
 
@@ -221,11 +221,11 @@
             visible = lax.broadcasted_iota(jnp.int32, (half, wide), 1) <= row + index % 2 * half
 
             def body(pair, carry):
-                for head in range(2):
-                    one_head(pair * 2 + head, blocks, visible)
+                for head in range(4):
+                    one_head(pair * 4 + head, blocks, visible)
                 return carry
 
-            lax.fori_loop(0, GROUPS // 2, body, 0)
+            lax.fori_loop(0, GROUPS // 4, body, 0)
 
 
 def attend(chunk, slots, own, queries, gathered, earlier):
@@ -285,6 +285,7 @@
     cosine = jnp.concatenate([cosine, cosine], axis=1)
     sine = jnp.concatenate([-sine, sine], axis=1)
 
+    hidden, incoming = lax.optimization_barrier((hidden, incoming))
     weights_new, *chunks = project(inverse, feature, hidden, cosine, sine, gathered)
     whole = [lax.all_gather(chunk, "ctx", axis=0, tiled=True) for chunk in chunks]
     first_new, second_new = ordered_moments(inverse, incoming)

time: 269 us -> 263 us (0.978)
  Pallas kernels: 58.8 us -> 53.2 us
  starting transfers between devices: 2.89 us -> 7.38 us
  local copies, waits for them, and re-layouts: 6.99 us -> 3.06 us
    all_gather x2 -> x1, waiting for transfers between devices: 18.3 us -> 59.4 us  [shards(): lax.all_gather(chunk, 'ctx', axis=0, tiled=True)]
    all_gather x1, waiting for transfers between devices: 116 us -> 86.8 us  [shards(): gathered = lax.all_gather(copies, both, axis=0, tiled=True)]
    all_to_all x1, waiting for transfers between devices: 45.9 us -> 34.1 us  [shards(): lax.all_to_all(outgoing, both, split_axis=0, concat_axis=0, tiled=True)]
    all_to_all x1, starting transfers between devices: 2.77 us -> 7.3 us  [shards(): lax.all_to_all(outgoing, both, split_axis=0, concat_axis=0, tiled=True)]
    unnamed x26 -> x14, local copies, waits for them, and re-layouts: 5.85 us -> 1.92 us
    pallas_call x2 -> x1, Pallas kernels: 37.9 us -> 34.1 us  [attend(): pl.pallas_call(functools.partial(attend_kernel, chunk), out_shape=jax.Sha...]
  transfers between devices with their start and end apart: 4 -> 3, of which waited for: 4 -> 3; matrix products, arithmetic and copies ran while one was open for 1% -> 1% of each run, Pallas kernels for 9% -> 2%
where the time goes in v2:
time: 263 us
  waiting for transfers between devices  180 us (68%)
  Pallas kernels  53.2 us (20%)
  between operations  14.2 us (5%)
  starting transfers between devices  7.38 us (3%)
  other arithmetic  5.16 us (2%)
  local copies, waits for them, and re-layouts  3.06 us (1%)
    all_gather x1, waiting for transfers between devices, shards(): gathered = lax.all_gather(copies, both, axis=0, tiled=True)  86.8 us
    all_gather x1, waiting for transfers between devices, shards(): lax.all_gather(chunk, 'ctx', axis=0, tiled=True)  59.4 us
    all_to_all x1, waiting for transfers between devices, shards(): lax.all_to_all(outgoing, both, split_axis=0, concat_axis=0, tiled=True)  34.1 us
    pallas_call x1, Pallas kernels, attend(): pl.pallas_call(functools.partial(attend_kernel, chunk), out_shape=jax.Sha...  34.1 us
    pallas_call x1, Pallas kernels, project(): pl.pallas_call(functools.partial(project_kernel, parts), out_shape=[jax.S...  14.6 us
    all_to_all x1, starting transfers between devices, shards(): lax.all_to_all(outgoing, both, split_axis=0, concat_axis=0, tiled=True)  7.3 us
  transfers between devices with their start and end apart: 3, of which 3 were waited for; matrix products, arithmetic and copies ran while one was open for 1% of the time, Pallas kernels for 2%

profile of v2, /device:TPU:0, one launch (start us, length us, event | category | flops | bytes accessed | tf_op | source)
XLA Modules:
  0.0 263.3 jit_solution(8624669326476272341)
XLA Ops:
  7.2 0.0 copy-start.1
  7.2 0.0 copy-start.2
  7.2 0.0 copy-start
  7.2 0.0 copy-start.3
  7.2 0.0 all-gather.3.cloned.1.call-start
  7.3 3.8 %fusion.7 = bf16[256,1024]{1,0:T(8,128)(2,1)} fusion(f32[256,1024]{1,0:T(8,128)} %param.11, f32[256,1024]{1,0:T(8,128)} %g_ref.1, f32[256,1024]{1,0:T(8,128)} %v_ref.1, f32[256,1024]{1,0:T(8,128)} %m_ref.1), kind=kLoop, calls=%fused_computation.8 | loop fusion | flops 3670016 | bytes 4718592 | tf_op jit(solution)/shard_map/convert_element_type | solution.py:268
  11.1 0.0 all-gather.3.cloned.1.call-update
  11.2 0.0 copy-start.5
  11.2 0.0 copy-start.6
  11.2 2.4 moments.1
  13.6 7.3 %all-to-all-start = ((bf16[32,64,256]{2,1,0:T(8,128)(2,1)}), bf16[32,64,256]{2,1,0:T(8,128)(2,1)S(1)}, u32[]{:S(2)}, u32[]{:S(2)}) async-start(bf16[32,64,256]{2,1,0:T(8,128)(2,1)} %moments.1), calls=%async_computation | async-start | bytes 2097152 | tf_op jit(solution)/shard_map/all_to_all | solution.py:271
  20.9 0.0 all-gather.5.cloned.1.call-start
  21.0 0.6 dynamic_slice.6.feature
  21.6 0.1 copy.23
  21.7 0.1 copy.24
  21.8 0.1 add_convert_fusion
  21.9 0.1 convert_element_type.14
  22.0 0.1 select_reduce_fusion.inverse
  22.1 0.8 fusion.8
  22.9 0.2 pad_maximum_fusion
  23.1 34.1 %all-to-all-done.in_ref = bf16[32,64,256]{2,1,0:T(8,128)(2,1)S(1)} async-done(((bf16[32,64,256]{2,1,0:T(8,128)(2,1)}), bf16[32,64,256]{2,1,0:T(8,128)(2,1)S(1)}, u32[]{:S(2)}, u32[]{:S(2)}) %all-to-all-start) | async-done | bytes 1048608 | tf_op jit(solution)/shard_map/all_to_all | solution.py:271
  57.2 86.8 %all-gather.3.cloned.1.call-done.refs_0_.refs_1_.refs_2_.refs_3_.refs_4_.refs_5_.refs_6_.refs_7_ = bf16[8192,1024]{1,0:T(8,128)(2,1)} async-done(((bf16[256,1024]{1,0:T(8,128)(2,1)}), bf16[8192,1024]{1,0:T(8,128)(2,1)}) %all-gather.3.cloned.1.call-update) | async-done | bytes 16777232 | tf_op jit(solution)/shard_map/all_gather | solution.py:269
  144.0 14.6 %project.1 = (f32[32,8192]{1,0:T(8,128)}, bf16[384,1024]{1,0:T(8,128)(2,1)}) custom-call(s32[32]{0:T(128)S(1)} %select_reduce_fusion.inverse, s32[1]{0:T(128)} %dynamic_slice.6.feature, bf16[1,384,8192]{2,1,0:T(8,128)(2,1)} %hidden_ref, f32[384,128]{1,0:T(8,128)S(1)} %get-tuple-element.21.cos_ref, f32[384,128]{1,0:T(8,128)S(1)} %get-tuple-element.22.sin_ref, ...), custom_call_target="tpu_custom_call" | custom-call | flops 6442450944 | bytes 23068672 | tf_op jit(solution)/shard_map/project/pallas_call | solution.py:150
  158.6 0.0 all-gather.5.cloned.1.call-update
  158.6 0.1 and.18
  158.7 0.1 copy.27
  158.8 0.1 div.24
  158.9 0.1 select_reduce_fusion.1.slots
  159.0 2.0 order.1
  161.0 59.4 %all-gather.5.cloned.1.call-done.kv_ref = bf16[1536,1024]{1,0:T(8,128)(2,1)} async-done(((bf16[384,1024]{1,0:T(8,128)(2,1)}), bf16[1536,1024]{1,0:T(8,128)(2,1)}) %all-gather.5.cloned.1.call-update) | async-done | bytes 3145744 | tf_op jit(solution)/shard_map/all_gather | solution.py:290
  220.5 1.9 copy-done.4
  222.3 34.1 %attend0.1 = bf16[1,384,4096]{2,1,0:T(8,128)(2,1)} custom-call(s32[8]{0:T(128)S(1)} %select_reduce_fusion.1.slots, s32[2]{0:T(128)S(1)} %get-tuple-element.17.own, bf16[1,384,4096]{2,1,0:T(8,128)(2,1)S(1)} %copy-done.4, bf16[1536,1024]{1,0:T(8,128)(2,1)} %all-gather.5.cloned.1.call-done.kv_ref), custom_call_target="tpu_custom_call" | custom-call | flops 9663676416 | bytes 6291456 | tf_op jit(solution)/shard_map/attend0/pallas_call | solution.py:240
  (14 shorter events, 0.1 us)
Async XLA Ops:
  7.2 4.0 %copy-start.1 = (f32[256,1024]{1,0:T(8,128)S(1)}, f32[256,1024]{1,0:T(8,128)}, u32[]{:S(2)}) copy-start(f32[256,1024]{1,0:T(8,128)} %v_ref.1) | copy-start | bytes 3145732
  7.2 4.0 %copy-start.2 = (f32[256,1024]{1,0:T(8,128)S(1)}, f32[256,1024]{1,0:T(8,128)}, u32[]{:S(2)}) copy-start(f32[256,1024]{1,0:T(8,128)} %m_ref.1) | copy-start | bytes 3145732
  7.2 4.0 %copy-start = (f32[256,1024]{1,0:T(8,128)S(1)}, f32[256,1024]{1,0:T(8,128)}, u32[]{:S(2)}) copy-start(f32[256,1024]{1,0:T(8,128)} %g_ref.1) | copy-start | bytes 3145732
  7.2 4.0 %copy-start.3 = (s32[32]{0:T(128)S(1)}, s32[32]{0:T(128)}, u32[]{:S(2)}) copy-start(s32[32]{0:T(128)} %new_owner.1) | copy-start | bytes 388
  7.2 136.8 %all-gather.3.cloned.1.call-start = ((), (), s32[]{:S(2)}) async-start(), calls=%async_computation.1 | async-start | bytes 17301504 | tf_op jit(solution)/shard_map/all_gather | solution.py:269
  11.2 10.4 %copy-start.5 = (s32[1,4,2]{1,2,0:T(2,128)S(1)}, s32[1,4,2]{1,2,0:T(2,128)}, u32[]{:S(2)}) copy-start(s32[1,4,2]{1,2,0:T(2,128)} %param.17) | copy-start | bytes 100
  11.2 10.8 %copy-start.6 = (s32[32]{0:T(128)S(1)}, s32[32]{0:T(128)}, u32[]{:S(2)}) copy-start(s32[32]{0:T(128)} %param.15) | copy-start | bytes 388
  13.6 43.6 %all-to-all-start = ((bf16[32,64,256]{2,1,0:T(8,128)(2,1)}), bf16[32,64,256]{2,1,0:T(8,128)(2,1)S(1)}, u32[]{:S(2)}, u32[]{:S(2)}) async-start(bf16[32,64,256]{2,1,0:T(8,128)(2,1)} %moments.1), calls=%async_computation | async-start | bytes 2097152 | tf_op jit(solution)/shard_map/all_to_all | solution.py:271
  20.9 199.5 %all-gather.5.cloned.1.call-start = ((), (), s32[]{:S(2)}) async-start(), calls=%async_computation.2 | async-start | bytes 3932160 | tf_op jit(solution)/shard_map/all_gather | solution.py:290
  220.5 1.9 copy-start.4
Sparse Core Ops, SparseCore 0:
  11.6 132.3 all-gather.2
  158.7 61.6 all-gather.4
